TPU v7x, 32 devices: a whole 2x2x4 slice. The times are simulated.
32 devices in a mesh: ctx: 16 (over z, x, core), ch: 2 (over y).
Axes of the slice: x: 2, y: 2, z: 4, core: 2. Of those that a mesh axis runs over, the one named last changes fastest.
Arguments:
- projections: bfloat16 [3, 4096, 8192], P(None, ('ctx', 'ch')), may hold values from -3 to 3
- attention_order: int32 [4096], replicated, may hold values from 0 to 4095, as said below
- doc_lengths: int32 [4], replicated, may hold values from 1 to 2048, 4096 in all
- short_filter: float32 [3, 3, 8192], P(None, None, 'ch'), may hold values from -3.5 to 3.5
- decay_rate: float32 [512, 16], P('ch'), may hold values from 2.4414063e-05 to 0.03
- residue: float32 [512, 16], P('ch'), may hold values from -1.5 to 1.5
- skip_gain: float32 [8192], P('ch'), may hold values from -2.5 to 2.5
Outputs:
- mixed_rows: bfloat16 [4096, 8192], P(('ctx', 'ch'))
Inputs may be any that keep to these rules, and one draw needn't show every extreme that they name: `attention_order`: A permutation of the 4096 positions. For every group a of 256 rows (rows a * 256 to (a + 1) * 256 - 1) and every context block j, the rows a * 256 + j * 16 to a * 256 + (j + 1) * 16 - 1 hold positions of block j, that is j * 256 to (j + 1) * 256 - 1, in any order. `doc_lengths`: the documents lie one after another in the slab; the lengths sum to 4096.
All inputs are finite; a program needn't handle non-finite values.
Results may differ from a plain program's by a relative error of at most 0.0049.
Values may be sent and summed in bfloat16 or wider, within the bound.
A program may use at most 128 MiB of HBM per device.

v0:
```python
import jax
import jax.numpy as jnp
from jax import lax
from jax.sharding import PartitionSpec as P

highest = lax.Precision.HIGHEST


def from_behind(value, axis, steps):
    count = lax.axis_size(axis)
    first, last = (max(0, -steps), min(count, count - steps))
    return lax.ppermute(value, axis, [(source, source + steps) for source in range(first, last)])


def entering(value, axis, combine, identity):
    devices, here = (lax.axis_size(axis), lax.axis_index(axis))
    everything = jax.tree.map(lambda part: lax.all_gather(part, axis), value)
    start = jax.tree.map(
        lambda part, zero: jnp.broadcast_to(jnp.asarray(zero, part.dtype), part.shape),
        value,
        identity,
    )

    def turn(k, before):
        reached = k < here
        new = combine(before, jax.tree.map(lambda part: part[k], everything))
        return jax.tree.map(lambda a, b: jnp.where(reached, a, b), new, before)

    return lax.fori_loop(0, devices, turn, start)


def doc_index(positions, bounds):
    return jnp.sum((positions[:, None] >= bounds[None, :]).astype(jnp.int32), axis=1)


def combine_states(earlier, later):
    return (earlier[0] * later[0], later[0] * earlier[1] + later[1])


def shards(projections, attention_order, doc_lengths, short_filter, decay_rate, residue, skip_gain):
    block_total = lax.axis_size("ctx")
    block_index = lax.axis_index("ctx")
    channels = short_filter.shape[2]
    row_count = projections.shape[1] * lax.axis_size("ch")
    slot_rows = row_count // block_total
    modes = decay_rate.shape[1]
    groups = decay_rate.shape[0]
    group_width = channels // groups
    first_row = block_index * row_count
    routing = attention_order.reshape(block_total, block_total, slot_rows)
    arrived = lax.dynamic_slice_in_dim(routing, block_index, 1, 1).reshape(row_count) - first_row
    placer = (arrived[None, :] == jnp.arange(row_count, dtype=jnp.int32)[:, None]).astype(
        jnp.bfloat16
    )
    received = lax.all_to_all(
        lax.all_to_all(projections, "ch", split_axis=2, concat_axis=1, tiled=True),
        "ctx",
        split_axis=1,
        concat_axis=1,
        tiled=True,
    )
    ordered = jnp.einsum(
        "tr,prc->ptc", placer, received, preferred_element_type=jnp.float32
    ).astype(jnp.bfloat16)
    earlier_rows = from_behind(ordered[:, row_count - 2 :, :], "ctx", 1)
    bounds = jnp.cumsum(doc_lengths)
    span_docs = doc_index(first_row - 2 + jnp.arange(row_count + 2, dtype=jnp.int32), bounds)
    current = span_docs[2:]
    previous_doc = span_docs[1]
    widened = jnp.concatenate([earlier_rows, ordered], axis=1)
    featured = jnp.zeros((3, row_count, channels), jnp.float32)
    for offset in range(3):
        same_doc = (span_docs[2 - offset : 2 - offset + row_count] == current).astype(jnp.float32)
        featured = (
            featured
            + short_filter[:, offset, None, :]
            * widened[:, 2 - offset : 2 - offset + row_count, :]
            * same_doc[None, :, None]
        )
    gated = lax.optimization_barrier((featured[1] * featured[2]).astype(jnp.bfloat16))
    coefficient = residue * jnp.sqrt(1.0 - jnp.exp(-2.0 * decay_rate))
    steps_float = jnp.arange(row_count, dtype=jnp.float32)
    tokens_index = jnp.arange(row_count, dtype=jnp.int32)
    causal = (
        (tokens_index[:, None] >= tokens_index[None, :]) & (current[:, None] == current[None, :])
    ).astype(jnp.float32)
    end_same = (current == current[row_count - 1]).astype(jnp.float32)
    carry_same = (current == previous_doc).astype(jnp.float32)
    group_batch = 8
    batch_count = groups // group_batch
    rate_blocks = decay_rate.reshape(batch_count, group_batch, modes)
    coeff_blocks = coefficient.reshape(batch_count, group_batch, modes)
    gated_blocks = jnp.moveaxis(
        gated.reshape(row_count, batch_count, group_batch * group_width), 1, 0
    )

    def local_block(inputs):
        rate_rows, coeffs, values = inputs
        values_wide = values.astype(jnp.float32).reshape(row_count, group_batch, group_width)
        falling = coeffs[:, :, None] * jnp.exp(-rate_rows[:, :, None] * steps_float[None, None, :])
        rising = jnp.exp(rate_rows[:, :, None] * steps_float[None, None, :])
        toeplitz = jnp.einsum("bmt,bms->bts", falling, rising, precision=highest) * causal[None]
        filtered_part = jnp.einsum("bts,sbc->tbc", toeplitz, values_wide, precision=highest)
        ending = (
            jnp.exp(-rate_rows[:, :, None] * (row_count - 1.0 - steps_float)[None, None, :])
            * end_same[None, None, :]
        )
        state_part = jnp.einsum("bms,sbc->mbc", ending, values_wide, precision=highest)
        return (
            filtered_part.reshape(row_count, group_batch * group_width),
            state_part.reshape(modes, group_batch * group_width),
        )

    filtered_blocks, state_blocks = lax.map(local_block, (rate_blocks, coeff_blocks, gated_blocks))
    filtered = jnp.moveaxis(filtered_blocks, 0, 1).reshape(row_count, channels)
    state_end = jnp.moveaxis(state_blocks, 0, 1).reshape(modes, channels)
    rate_wide = jnp.repeat(decay_rate.T, group_width, axis=1)
    linking = (previous_doc == current[row_count - 1]).astype(jnp.float32)
    factor = jnp.exp(-rate_wide * row_count) * linking
    carried = entering(
        (factor, state_end),
        "ctx",
        combine_states,
        (jnp.ones_like(factor), jnp.zeros_like(state_end)),
    )[1]
    reaching = coefficient[:, :, None] * jnp.exp(
        -decay_rate[:, :, None] * (steps_float + 1.0)[None, None, :]
    )
    incoming = jnp.einsum(
        "gmt,mgc->tgc", reaching, carried.reshape(modes, groups, group_width), precision=highest
    ).reshape(row_count, channels)
    combined = (
        filtered + incoming * carry_same[:, None] + skip_gain[None, :] * gated.astype(jnp.float32)
    )
    mixed = (featured[0] * combined).astype(jnp.bfloat16)
    returned = jnp.einsum("tr,tc->rc", placer, mixed, preferred_element_type=jnp.float32).astype(
        jnp.bfloat16
    )
    return lax.all_to_all(
        lax.all_to_all(returned, "ctx", split_axis=0, concat_axis=0, tiled=True),
        "ch",
        split_axis=0,
        concat_axis=1,
        tiled=True,
    )


def solution(mesh):
    placed = (
        P(None, ("ctx", "ch"), None),
        P(),
        P(),
        P(None, None, "ch"),
        P("ch", None),
        P("ch", None),
        P("ch"),
    )
    return jax.shard_map(
        shards, mesh=mesh, in_specs=placed, out_specs=P(("ctx", "ch"), None), check_vma=False
    )
```

profile of v0, /device:TPU:0, one launch (start us, length us, event | category | flops | bytes accessed | tf_op | source)
XLA Modules:
  0.0 762.3 jit_solution(6097198763027492637)
XLA Ops:
  6.5 13.2 %copy.56 = bf16[3,128,8192]{1,0,2:T(4,128)(2,1)} copy(bf16[3,128,8192]{2,1,0:T(8,128)(2,1)} %param.11) | data formatting | bytes 12582912 | tf_op args[0]
  19.7 104.8 %all_to_all.51 = bf16[3,128,8192]{1,0,2:T(4,128)(2,1)} all-to-all(bf16[3,128,8192]{1,0,2:T(4,128)(2,1)} %copy.56), channel_id=1, replica_groups=mesh['ctx'=16,'ch'=2] {'ch'}, dimensions={2} | all-to-all | bytes 12582912 | tf_op jit(solution)/shard_map/all_to_all | solution.py:56
  124.5 17.6 %copy.57 = bf16[3,2,128,4096]{3,0,2,1:T(4,128)(2,1)} copy(bf16[3,2,128,4096]{2,0,3,1:T(4,128)(2,1)} %bitcast.91) | data formatting | bytes 12582912 | tf_op jit(solution)/shard_map/all_to_all | solution.py:56
  142.2 6.3 all-to-all-start.1
  151.4 2.3 mul.231
  154.2 170.4 %all-to-all-done.1 = bf16[3,256,4096]{2,0,1:T(4,128)(2,1)} async-done(((bf16[3,256,4096]{2,0,1:T(4,128)(2,1)}), bf16[3,256,4096]{2,0,1:T(4,128)(2,1)}, u32[]{:S(2)}, u32[]{:S(2)}) %all-to-all-start.1) | async-done | bytes 6291488 | tf_op jit(solution)/shard_map/all_to_all | solution.py:55
  324.6 11.1 %fusion.28 = bf16[3,256,4096]{2,1,0:T(8,128)(2,1)S(1)} fusion(bf16[3,256,4096]{2,0,1:T(4,128)(2,1)} %all-to-all-done.1, s32[256]{0:T(256)S(1)} %sub.31), kind=kOutput, calls=%fused_computation.40 | convolution fusion | flops 1613824000 | bytes 12583936 | tf_op jit(solution)/shard_map/tr,prc->ptc/dot_general | solution.py:62
  335.7 2.7 copy-done.1
  338.4 2.9 collective-permute-start
  341.2 1.3 compare_convert_fusion
  342.9 10.5 %multiply_add_fusion = f32[3,256,4096]{2,1,0:T(8,128)S(1)} fusion(bf16[3,256,4096]{2,1,0:T(8,128)(2,1)} %copy-done.1, bf16[3,2,4096]{2,1,0:T(2,128)(2,1)S(1)} %collective-permute-done, f32[256]{0:T(256)S(1)} %get-tuple-element.253, f32[3,4096]{1,0:T(4,128)S(1)} %get-tuple-element.257, f32[256]{0:T(256)S(1)} %get-tuple-element.254, ...), kind=kLoop, calls=%fused_computation.33 | loop fusion | flops 50331648 | bytes 19073024 | tf_op jit(solution)/shard_map/add | solution.py:75
  353.4 4.5 copy-done
  358.4 2.5 copy.70
  360.9 182.2 %while.28 = (s32[]{:T(128)}, f32[32,256,128]{1,2,0:T(8,128)}, f32[32,16,128]{1,2,0:T(8,128)}, bf16[32,256,128]{1,2,0:T(8,128)(2,1)}, f32[32,8,16]{2,1,0:T(8,128)...) while((s32[]{:T(128)}, f32[32,256,128]{1,2,0:T(8,128)}, ...), condition=%wide.region_3.4_spmd.clone.clone, body=%wide.region_2.3_spmd.clone.clone.sunk | while | flops 208568704 | bytes 5465705 | solution.py:114
  360.9 2.0 fusion.75
  366.6 2.0 fusion.75
  372.3 2.0 fusion.75
  378.0 2.0 fusion.75
  383.7 2.0 fusion.75
  389.4 2.0 fusion.75
  395.1 2.0 fusion.75
  400.8 2.0 fusion.75
  406.5 2.0 fusion.75
  412.2 2.0 fusion.75
  417.9 2.0 fusion.75
  423.6 2.0 fusion.75
  429.3 2.0 fusion.75
  435.0 2.0 fusion.75
  440.7 2.0 fusion.75
  446.4 2.0 fusion.75
  452.1 2.0 fusion.75
  457.8 2.0 fusion.75
  463.5 2.0 fusion.75
  469.2 2.0 fusion.75
  474.9 2.0 fusion.75
  480.6 2.0 fusion.75
  486.2 2.0 fusion.75
  491.9 2.0 fusion.75
  497.6 2.0 fusion.75
  503.3 2.0 fusion.75
  509.0 2.0 fusion.75
  514.7 2.0 fusion.75
  520.4 2.0 fusion.75
  526.1 2.0 fusion.75
  531.8 2.0 fusion.75
  537.5 2.0 fusion.75
  543.2 2.9 copy.72
  546.2 5.7 copy.71
  551.9 77.0 %all-gather.5.cloned.1.call-done = f32[16,16,4096]{2,1,0:T(8,128)} async-done(((f32[1,16,4096]{2,1,0:T(8,128)}), f32[16,16,4096]{2,1,0:T(8,128)}) %all-gather.5.cloned.1.call-update) | async-done | bytes 4194320 | tf_op jit(solution)/shard_map/all_gather | solution.py:17
  628.9 20.3 %while.29 = (s32[]{:T(128)}, f32[16,4096]{1,0:T(8,128)S(1)}, s32[]{:T(128)}, f32[16,16,4096]{2,1,0:T(8,128)}, f32[16,16,4096]{2,1,0:T(8,128)}, /*index=5*/s32[]{:T(128)}, s32[]{:T(128)}) while((s32[]{:T(128)}, f32[16,4096]{1,0:T(8,128)S(1)}, s32[]{:T(128)}, f32[16,16,4096]{2,1,0:T(8,128)}, f32[16,16,4096]{2,1,0:T(8,128)}, ...), condition=%wide.region_5.6_spmd.clone, body=%wide.region_4.5_spmd.clone.sunk | while | flops 262148 | bytes 1048677 | solution.py:29
  630.2 1.2 fusion.79
  631.5 1.2 fusion.79
  632.7 1.2 fusion.79
  634.0 1.2 fusion.79
  635.3 1.2 fusion.79
  636.6 1.2 fusion.79
  649.3 1.9 copy.73
  651.2 7.1 fusion.34
  658.3 5.7 copy.67
  664.0 6.0 convolution_convert_fusion.1
  670.0 50.3 %all_to_all.52 = bf16[16,16,4096]{2,1,0:T(8,128)(2,1)S(1)} all-to-all(bf16[16,16,4096]{2,1,0:T(8,128)(2,1)S(1)} %bitcast.97), channel_id=1, replica_groups=mesh['ctx'=16,'ch'=2] {'ctx'}, dimensions={0} | all-to-all | bytes 4194304 | tf_op jit(solution)/shard_map/all_to_all | solution.py:140
  720.3 28.6 %all_to_all.53 = bf16[2,128,4096]{2,1,0:T(8,128)(2,1)S(1)} all-to-all(bf16[2,128,4096]{2,1,0:T(8,128)(2,1)S(1)} %bitcast.95), channel_id=1, replica_groups=mesh['ctx'=16,'ch'=2] {'ch'}, dimensions={0} | all-to-all | bytes 4194304 | tf_op jit(solution)/shard_map/all_to_all | solution.py:139
  748.9 2.5 copy.68
  751.4 4.1 copy.69
  (340 shorter events, 133.6 us)
Async XLA Ops:
  142.2 6.4 copy-start.7
  142.2 8.6 %copy-start.3 = (f32[256,16]{0,1:T(8,128)S(1)}, f32[256,16]{0,1:T(8,128)}, u32[]{:S(2)}) copy-start(f32[256,16]{0,1:T(8,128)} %param.15) | copy-start | bytes 49156
  142.2 8.6 %copy-start.4 = (f32[256,16]{0,1:T(8,128)S(1)}, f32[256,16]{0,1:T(8,128)}, u32[]{:S(2)}) copy-start(f32[256,16]{0,1:T(8,128)} %param.16) | copy-start | bytes 49156
  142.2 182.4 %all-to-all-start.1 = ((bf16[3,256,4096]{2,0,1:T(4,128)(2,1)}), bf16[3,256,4096]{2,0,1:T(4,128)(2,1)}, u32[]{:S(2)}, u32[]{:S(2)}) async-start(bf16[3,256,4096]{2,0,1:T(4,128)(2,1)} %bitcast.90), calls=%async_computation.1 | async-start | bytes 16777216 | tf_op jit(solution)/shard_map/all_to_all | solution.py:55
  148.5 5.3 copy-start.5
  148.5 5.5 copy-start.2
  148.5 403.3 %all-gather.3.cloned.1.call-start = ((), (), s32[]{:S(2)}) async-start(), calls=%async_computation.4 | async-start | bytes 4456448 | tf_op jit(solution)/shard_map/all_gather | solution.py:17
  153.7 475.2 %all-gather.5.cloned.1.call-start = ((), (), s32[]{:S(2)}) async-start(), calls=%async_computation.5 | async-start | bytes 4456448 | tf_op jit(solution)/shard_map/all_gather | solution.py:17
  335.7 2.7 copy-start.1
  338.4 4.5 collective-permute-start
  353.4 4.5 copy-start
  658.3 5.7 copy-start.6
Sparse Core Ops, SparseCore 0:
  153.8 147.6 all-gather.2
  546.2 82.6 all-gather.4
where the time goes:
time: 766 us; the launch traced here: 762 us
  waiting for transfers between devices  247 us (32%)
  blocking collectives  184 us (24%)
  local copies, waits for them, and re-layouts  137 us (18%)
  matrix products  133 us (17%)
  other arithmetic  36.1 us (5%)
  between operations  14.9 us (2%)
  starting transfers between devices  9.27 us (1%)
    all_to_all x1, waiting for transfers between devices, shards(): lax.all_to_all(lax.all_to_all(projections, 'ch', split_axis=2, concat_axi...  170 us
    all_to_all x1, blocking collectives, shards(): lax.all_to_all(projections, 'ch', split_axis=2, concat_axis=1, tiled=True)  105 us
    all_gather x2, waiting for transfers between devices, entering(): everything = jax.tree.map(lambda part: lax.all_gather(part, axis), value)  77 us
    dot_general x32, matrix products, local_block(): jnp.einsum('bmt,bms->bts', falling, rising, precision=highest)  63.3 us
    all_to_all x1, blocking collectives, shards(): lax.all_to_all(returned, 'ctx', split_axis=0, concat_axis=0, tiled=True)  50.3 us
    dynamic_update_slice x64, local copies, waits for them, and re-layouts, shards(): lax.map(local_block, (rate_blocks, coeff_blocks, gated_blocks))  42 us
    dot_general x32, matrix products, local_block(): jnp.einsum('bts,sbc->tbc', toeplitz, values_wide, precision=highest)  36.2 us
    all_to_all x1, blocking collectives, shards(): lax.all_to_all(lax.all_to_all(returned, 'ctx', split_axis=0, concat_axis=...  28.6 us
  transfers between devices with their start and end apart: 4, of which 2 were waited for; matrix products, arithmetic and copies ran while one was open for 29% of the time, Pallas kernels for 0%

commit v1 on v0

--- a/solution.py
+++ b/solution.py
@@ -1,7 +1,13 @@
+import functools
+
 import jax
 import jax.numpy as jnp
 from jax import lax
+from jax.experimental import pallas as pl
+from jax.experimental.pallas import tpu as pltpu
 from jax.sharding import PartitionSpec as P
+
+LANES = 128
 
 highest = lax.Precision.HIGHEST
 
@@ -37,7 +43,7 @@
     return (earlier[0] * later[0], later[0] * earlier[1] + later[1])
 
 
-def shards(projections, attention_order, doc_lengths, short_filter, decay_rate, residue, skip_gain):
+def block_shards(projections, attention_order, doc_lengths, short_filter, decay_rate, residue, skip_gain):
     block_total = lax.axis_size("ctx")
     block_index = lax.axis_index("ctx")
     channels = short_filter.shape[2]
@@ -63,7 +69,7 @@
         "tr,prc->ptc", placer, received, preferred_element_type=jnp.float32
     ).astype(jnp.bfloat16)
     earlier_rows = from_behind(ordered[:, row_count - 2 :, :], "ctx", 1)
-    bounds = jnp.cumsum(doc_lengths)
+    bounds = jnp.sum(jnp.tril(jnp.broadcast_to(doc_lengths, (doc_lengths.size,) * 2)), axis=1)
     span_docs = doc_index(first_row - 2 + jnp.arange(row_count + 2, dtype=jnp.int32), bounds)
     current = span_docs[2:]
     previous_doc = span_docs[1]
@@ -145,6 +151,370 @@
     )
 
 
+def doc_of(positions, bounds):
+    found = jnp.zeros(positions.shape, jnp.int32) if positions.shape else jnp.int32(0)
+    for bound in bounds:
+        found = found + (positions >= bound).astype(jnp.int32)
+    return found
+
+
+def channel_kernel(
+    sizes,
+    projections,
+    order,
+    lengths,
+    short_filter,
+    skip_gain,
+    rates,
+    coefficients,
+    rate_rows,
+    out,
+    held,
+    back,
+    placers,
+    returners,
+    toeplitz,
+    endings,
+    reaching,
+    gate,
+    query,
+    sources,
+    filtered,
+    doc_masks,
+    end_mask,
+    carry_mask,
+    local_sems,
+    there_send,
+    there_recv,
+    home_send,
+    home_recv,
+):
+    blocks, shares, length, slot, fold, chunks, filters, modes = sizes
+    devices = blocks * shares
+    rows = length // shares
+    slots = rows // slot
+    per_chunk = LANES // fold
+    width = chunks * LANES
+    docs = lengths.shape[0]
+    channels = short_filter.shape[2]
+    ctx = lax.axis_index("ctx")
+    here = ctx * shares + lax.axis_index("ch")
+    own_columns = ctx * width
+
+    def place(device):
+        return {"ctx": device // shares, "ch": device % shares}
+
+    def first_column(device, chunk):
+        first = (device % shares) * channels + (device // shares) * width + chunk * LANES
+        return pl.multiple_of(first, LANES)
+
+    def there(chunk, target, source):
+        return pltpu.make_async_remote_copy(
+            src_ref=projections.at[:, :, pl.ds(first_column(target, chunk), LANES)],
+            dst_ref=held.at[chunk, source],
+            send_sem=there_send.at[chunk, target],
+            recv_sem=there_recv.at[chunk, source],
+            device_id=place(target),
+            device_id_type=pl.DeviceIdType.MESH,
+        )
+
+    def home(chunk, target, source):
+        return pltpu.make_async_remote_copy(
+            src_ref=back.at[chunk, target],
+            dst_ref=out.at[:, pl.ds(first_column(source, chunk), LANES)],
+            send_sem=home_send.at[chunk, target],
+            recv_sem=home_recv.at[chunk, source],
+            device_id=place(target),
+            device_id_type=pl.DeviceIdType.MESH,
+        )
+
+    def local_there(chunk):
+        return pltpu.make_async_copy(
+            projections.at[:, :, pl.ds(first_column(here, chunk), LANES)],
+            held.at[chunk, here],
+            local_sems.at[0, chunk],
+        )
+
+    def local_home(chunk):
+        return pltpu.make_async_copy(
+            back.at[chunk, here],
+            out.at[:, pl.ds(first_column(here, chunk), LANES)],
+            local_sems.at[1, chunk],
+        )
+
+    def others(act):
+        def turn(step, carry):
+            act((here + step) % devices)
+            return carry
+
+        lax.fori_loop(1, devices, turn, 0)
+
+    barrier = pltpu.get_barrier_semaphore()
+    others(
+        lambda device: pl.semaphore_signal(
+            barrier, inc=1, device_id=place(device), device_id_type=pl.DeviceIdType.MESH
+        )
+    )
+    pl.semaphore_wait(barrier, devices - 1)
+    for chunk in range(chunks):
+        others(lambda device: there(chunk, device, here).start())
+        local_there(chunk).start()
+
+    bounds = []
+    total = jnp.int32(0)
+    for index in range(docs):
+        total = total + lengths[index]
+        bounds.append(total)
+
+    square = (length, length)
+    down = lax.broadcasted_iota(jnp.int32, square, 0)
+    across = lax.broadcasted_iota(jnp.int32, square, 1)
+
+    def make_placers(block, carry):
+        placer = (order[block] == down).astype(jnp.float32)
+        placers[block] = placer.astype(jnp.bfloat16)
+        returners[block] = placer.T.astype(jnp.bfloat16)
+        return carry
+
+    lax.fori_loop(0, blocks, make_placers, 0)
+
+    steps = lax.broadcasted_iota(jnp.int32, (modes, length), 1).astype(jnp.float32)
+
+    def split(value):
+        high = value.astype(jnp.bfloat16)
+        low = (value - high.astype(jnp.float32)).astype(jnp.bfloat16)
+        return high, low
+
+    def make_filters(index, carry):
+        rate = rates[index]
+        falling = coefficients[index] * jnp.exp(-rate * steps)
+        impulse = jnp.sum(falling, axis=0, keepdims=True)
+        turned = pltpu.roll(
+            jnp.broadcast_to(impulse, square), 0, axis=1, stride=1, stride_axis=0
+        )
+        toeplitz[index] = jnp.where(across >= down, turned, 0.0).astype(jnp.bfloat16)
+        high, low = split(jnp.exp(-rate * (length - 1.0 - steps)))
+        endings[index, 0] = jnp.concatenate([high, high, high], axis=0)
+        endings[index, 1] = jnp.concatenate([low, low, low], axis=0)
+        high, low = split(coefficients[index] * jnp.exp(-rate * (steps + 1.0)))
+        reaching[index] = jnp.concatenate([high, high, low], axis=0)
+        return carry
+
+    lax.fori_loop(0, filters, make_filters, 0)
+
+    strip = (blocks * fold, length)
+    strip_block = lax.broadcasted_iota(jnp.int32, strip, 0) // fold
+    strip_doc = doc_of(strip_block * length + lax.broadcasted_iota(jnp.int32, strip, 1), bounds)
+    for doc in range(docs):
+        doc_masks[doc] = (strip_doc == doc).astype(jnp.float32)
+    last_doc = doc_of(strip_block * length + (length - 1), bounds)
+    end_mask[...] = (strip_doc == last_doc).astype(jnp.bfloat16)
+    first_doc = doc_of(strip_block * length - 1, bounds)
+    carry_mask[...] = (strip_doc == first_doc).astype(jnp.float32)
+
+    tile = (length, LANES)
+    tile_rows = lax.broadcasted_iota(jnp.int32, tile, 0)
+    lane = lax.broadcasted_iota(jnp.int32, (blocks * fold, 3 * modes), 1)
+    middle = (lane >= modes) & (lane < 2 * modes)
+
+    def fresh(positions):
+        found = positions == 0
+        for bound in bounds[:-1]:
+            found = found | (positions == bound)
+        return found
+
+    def work(chunk):
+        columns = pl.ds(pl.multiple_of(own_columns + chunk * LANES, LANES), LANES)
+        taps = [[short_filter[j, tap : tap + 1, columns] for tap in range(3)] for j in range(3)]
+        skip = skip_gain[:, columns]
+        grouped = held.at[chunk]
+
+        def gather(block, tails):
+            share, inner = block // slots, block % slots
+            at = pl.ds(pl.multiple_of(inner * slot, slot), slot)
+            positions = block * length + tile_rows
+            keep_one = jnp.where(fresh(positions), 0.0, 1.0)
+            keep_two = jnp.where(fresh(positions - 1), 0.0, keep_one)
+            placer = placers[block]
+            featured, new_tails = [], []
+            for j in range(3):
+                arrived = jnp.concatenate(
+                    [grouped[a * shares + share, j, at, :] for a in range(blocks)], axis=0
+                )
+                ordered = jnp.dot(placer, arrived, preferred_element_type=jnp.float32)
+                longer = jnp.concatenate([tails[j], ordered], axis=0)
+                featured.append(
+                    taps[j][0] * ordered
+                    + taps[j][1] * longer[7 : 7 + length] * keep_one
+                    + taps[j][2] * longer[6 : 6 + length] * keep_two
+                )
+                new_tails.append(ordered[length - 8 :])
+            product = (featured[1] * featured[2]).astype(jnp.bfloat16)
+            query[block] = featured[0]
+            gate[block] = product
+            turned = product.astype(jnp.float32).T.astype(jnp.bfloat16)
+            to = pl.ds(pl.multiple_of(block * fold, fold), fold)
+            for group in range(per_chunk):
+                sources[group, to, :] = turned[group * fold : (group + 1) * fold]
+            return tuple(new_tails)
+
+        lax.fori_loop(
+            0, blocks, gather, tuple(jnp.zeros((8, LANES), jnp.float32) for _ in range(3))
+        )
+
+        def convolve(group, carry):
+            index = chunk * per_chunk + group
+            values = sources[group]
+            kernel_rows = toeplitz[index]
+            ended = values * end_mask[...]
+            contract = (((1,), (1,)), ((), ()))
+            states = lax.dot_general(
+                ended, endings[index, 0], contract, preferred_element_type=jnp.float32
+            ) + lax.dot_general(
+                ended, endings[index, 1], contract, preferred_element_type=jnp.float32
+            )
+            factor = jnp.exp(-rate_rows[index] * float(length))
+            state = jnp.zeros((fold, 3 * modes), jnp.float32)
+            entering_states = []
+            for block in range(blocks):
+                entering_states.append(state)
+                before = doc_of(jnp.int32(block * length - 1), bounds)
+                after = doc_of(jnp.int32(block * length + length - 1), bounds)
+                linked = (before == after).astype(jnp.float32)
+                state = factor * linked * state + states[block * fold : (block + 1) * fold]
+            entered = jnp.concatenate(entering_states, axis=0)
+            high = entered.astype(jnp.bfloat16).astype(jnp.float32)
+            parts = jnp.where(middle, entered - high, high).astype(jnp.bfloat16)
+            total = carry_mask[...] * jnp.dot(
+                parts, reaching[index], preferred_element_type=jnp.float32
+            )
+            for doc in range(docs):
+                mask = doc_masks[doc]
+                total = total + mask * jnp.dot(
+                    values * mask.astype(jnp.bfloat16),
+                    kernel_rows,
+                    preferred_element_type=jnp.float32,
+                )
+            at = pl.ds(pl.multiple_of(group * fold, fold), fold)
+            for block in range(blocks):
+                filtered[block, at, :] = total[block * fold : (block + 1) * fold]
+            return carry
+
+        lax.fori_loop(0, per_chunk, convolve, 0)
+
+        def mix(block, carry):
+            share, inner = block // slots, block % slots
+            at = pl.ds(pl.multiple_of(inner * slot, slot), slot)
+            combined = filtered[block].T + skip * gate[block].astype(jnp.float32)
+            mixed = (query[block] * combined).astype(jnp.bfloat16)
+            returned = jnp.dot(
+                returners[block], mixed, preferred_element_type=jnp.float32
+            ).astype(jnp.bfloat16)
+            for a in range(blocks):
+                back[chunk, a * shares + share, at, :] = returned[a * slot : (a + 1) * slot]
+            return carry
+
+        lax.fori_loop(0, blocks, mix, 0)
+
+    for chunk in range(chunks):
+        others(lambda device: there(chunk, here, device).wait_recv())
+        local_there(chunk).wait()
+        work(chunk)
+        others(lambda device: home(chunk, device, here).start())
+        local_home(chunk).start()
+    for chunk in range(chunks):
+        others(lambda device: there(chunk, device, here).wait_send())
+        others(lambda device: home(chunk, device, here).wait_send())
+        others(lambda device: home(chunk, here, device).wait_recv())
+        local_home(chunk).wait()
+
+
+def channel_shards(
+    projections, attention_order, doc_lengths, short_filter, decay_rate, residue, skip_gain
+):
+    blocks, shares = lax.axis_size("ctx"), lax.axis_size("ch")
+    devices = blocks * shares
+    rows, model = projections.shape[1:]
+    length = rows * shares
+    slot = length // blocks
+    channels = short_filter.shape[2]
+    groups, modes = decay_rate.shape
+    fold = channels // groups
+    width = model // devices
+    chunks = width // LANES
+    filters = width // fold
+    docs = doc_lengths.shape[0]
+    coefficient = residue * jnp.sqrt(1.0 - jnp.exp(-2.0 * decay_rate))
+    first = lax.axis_index("ctx") * filters
+    rates = lax.dynamic_slice_in_dim(decay_rate, first, filters, 0)
+    coefficients = lax.dynamic_slice_in_dim(coefficient, first, filters, 0)
+    order = attention_order.reshape(blocks, blocks, slot).transpose(1, 0, 2)
+    order = order.reshape(blocks, 1, length)
+    order = order - (jnp.arange(blocks, dtype=jnp.int32) * length)[:, None, None]
+    sizes = (blocks, shares, length, slot, fold, chunks, filters, modes)
+    vmem = pl.BlockSpec(memory_space=pltpu.VMEM)
+    strip = (blocks * fold, length)
+    per_chunk = LANES // fold
+    return pl.pallas_call(
+        functools.partial(channel_kernel, sizes),
+        out_shape=jax.ShapeDtypeStruct((rows, model), jnp.bfloat16),
+        in_specs=[
+            pl.BlockSpec(memory_space=pl.ANY),
+            vmem,
+            pl.BlockSpec(memory_space=pltpu.SMEM),
+            vmem,
+            vmem,
+            vmem,
+            vmem,
+            vmem,
+        ],
+        out_specs=pl.BlockSpec(memory_space=pl.ANY),
+        scratch_shapes=[
+            pltpu.VMEM((chunks, devices, 3, rows, LANES), jnp.bfloat16),
+            pltpu.VMEM((chunks, devices, rows, LANES), jnp.bfloat16),
+            pltpu.VMEM((blocks, length, length), jnp.bfloat16),
+            pltpu.VMEM((blocks, length, length), jnp.bfloat16),
+            pltpu.VMEM((filters, length, length), jnp.bfloat16),
+            pltpu.VMEM((filters, 2, 3 * modes, length), jnp.bfloat16),
+            pltpu.VMEM((filters, 3 * modes, length), jnp.bfloat16),
+            pltpu.VMEM((blocks, length, LANES), jnp.bfloat16),
+            pltpu.VMEM((blocks, length, LANES), jnp.float32),
+            pltpu.VMEM((per_chunk,) + strip, jnp.bfloat16),
+            pltpu.VMEM((blocks, LANES, length), jnp.float32),
+            pltpu.VMEM((docs,) + strip, jnp.float32),
+            pltpu.VMEM(strip, jnp.bfloat16),
+            pltpu.VMEM(strip, jnp.float32),
+            pltpu.SemaphoreType.DMA((2, chunks)),
+            pltpu.SemaphoreType.DMA((chunks, devices)),
+            pltpu.SemaphoreType.DMA((chunks, devices)),
+            pltpu.SemaphoreType.DMA((chunks, devices)),
+            pltpu.SemaphoreType.DMA((chunks, devices)),
+        ],
+        compiler_params=pltpu.CompilerParams(
+            collective_id=0, has_side_effects=True, vmem_limit_bytes=48 * 1024 * 1024
+        ),
+    )(
+        projections,
+        order,
+        doc_lengths,
+        short_filter,
+        skip_gain[None, :],
+        rates[:, :, None],
+        coefficients[:, :, None],
+        jnp.tile(rates, (1, 3))[:, None, :],
+    )
+
+
+def shards(projections, attention_order, doc_lengths, short_filter, decay_rate, residue, skip_gain):
+    devices = lax.axis_size("ctx") * lax.axis_size("ch")
+    slot = projections.shape[1] * lax.axis_size("ch") // lax.axis_size("ctx")
+    whole_tiles = projections.shape[2] % (devices * LANES) == 0 and slot % 16 == 0
+    run = channel_shards if whole_tiles else block_shards
+    return run(
+        projections, attention_order, doc_lengths, short_filter, decay_rate, residue, skip_gain
+    )
+
+
 def solution(mesh):
     placed = (
         P(None, ("ctx", "ch"), None),

time: 766 us -> 211 us (0.28)
  the two profiles are of different devices: /device:TPU:0 before, /device:TPU:19 now
where the time goes in v1:
time: 211 us
  Pallas kernels  204 us (97%)
  local copies, waits for them, and re-layouts  5.09 us (2%)
    pallas_call x1, Pallas kernels, channel_shards(): pl.pallas_call(functools.partial(channel_kernel, sizes), out_shape=jax.Sh...  204 us

profile of v1, /device:TPU:19, one launch (start us, length us, event | category | flops | bytes accessed | tf_op | source)
XLA Modules:
  0.0 210.5 jit_solution(15359167445357687290)
XLA Ops:
  0.0 0.8 fusion
  0.8 0.1 copy.28
  0.9 0.1 tile.9
  1.0 0.2 copy.24.coefficients
  1.2 0.2 copy.23.rates
  1.3 0.8 reshape.49
  2.2 0.1 reshape.50
  2.3 0.1 broadcast_subtract_fusion.order
  2.4 0.0 copy-start
  2.4 0.9 copy-done
  3.3 0.0 copy-start.1
  3.3 0.7 copy-done.1
  4.0 0.0 copy-start.2
  4.0 0.7 copy-done.2
  4.7 204.5 %shard_map.73 = bf16[128,8192]{1,0:T(8,128)(2,1)S(1)} custom-call(bf16[3,128,8192]{2,1,0:T(8,128)(2,1)} %projections.1, s32[16,1,256]{2,1,0:T(1,128)S(1)} %broadcast_subtract_fusion.order, s32[4]{0:T(128)S(1)} %copy-done.2, f32[3,3,4096]{2,1,0:T(4,128)S(1)} %copy-done, f32[1,4096]{1,0:T(1,128)S(1)} %bitcast.7, f32[16,16,1]{2,1,0:T(8,128)S(1)} %copy.23.rates, ...), custom_call_target="tpu_custom_call" | custom-call | tf_op jit(solution)/shard_map/pallas_call | solution.py:458
  209.2 1.3 copy.30
  (3 shorter events, 0.1 us)
Async XLA Ops:
  2.4 0.9 copy-start
  3.3 0.7 copy-start.1
  4.0 0.7 copy-start.2

commit v2 on v1

--- a/solution.py
+++ b/solution.py
@@ -1,4 +1,5 @@
 import functools
+import math
 
 import jax
 import jax.numpy as jnp
@@ -242,9 +243,11 @@
             local_sems.at[1, chunk],
         )
 
+    stride = devices // 2 - 3 if math.gcd(devices // 2 - 3, devices) == 1 else 1
+
     def others(act):
         def turn(step, carry):
-            act((here + step) % devices)
+            act((here + step * stride) % devices)
             return carry
 
         lax.fori_loop(1, devices, turn, 0)

time: 211 us -> 202 us (0.957)
  the two profiles are of different devices: /device:TPU:19 before, /device:TPU:0 now
where the time goes in v2:
time: 202 us; the launch traced here: 200 us
  Pallas kernels  194 us (96%)
  local copies, waits for them, and re-layouts  5.09 us (3%)
    pallas_call x1, Pallas kernels, channel_shards(): pl.pallas_call(functools.partial(channel_kernel, sizes), out_shape=jax.Sh...  194 us

profile of v2, /device:TPU:0, one launch (start us, length us, event | category | flops | bytes accessed | tf_op | source)
XLA Modules:
  0.0 199.7 jit_solution(9292960244504565751)
XLA Ops:
  0.0 0.8 fusion
  0.8 0.1 copy.28
  0.9 0.1 tile.9
  1.0 0.2 copy.24.coefficients
  1.2 0.2 copy.23.rates
  1.3 0.8 reshape.49
  2.2 0.1 reshape.50
  2.3 0.1 broadcast_subtract_fusion.order
  2.4 0.0 copy-start
  2.4 0.9 copy-done
  3.3 0.0 copy-start.1
  3.3 0.7 copy-done.1
  4.0 0.0 copy-start.2
  4.0 0.7 copy-done.2
  4.7 193.7 %shard_map.73 = bf16[128,8192]{1,0:T(8,128)(2,1)S(1)} custom-call(bf16[3,128,8192]{2,1,0:T(8,128)(2,1)} %projections.1, s32[16,1,256]{2,1,0:T(1,128)S(1)} %broadcast_subtract_fusion.order, s32[4]{0:T(128)S(1)} %copy-done.2, f32[3,3,4096]{2,1,0:T(4,128)S(1)} %copy-done, f32[1,4096]{1,0:T(1,128)S(1)} %bitcast.7, f32[16,16,1]{2,1,0:T(8,128)S(1)} %copy.23.rates, ...), custom_call_target="tpu_custom_call" | custom-call | tf_op jit(solution)/shard_map/pallas_call | solution.py:461
  198.4 1.3 copy.30
  (3 shorter events, 0.1 us)
Async XLA Ops:
  2.4 0.9 copy-start
  3.3 0.7 copy-start.1
  4.0 0.7 copy-start.2

commit v3 on v2

--- a/solution.py
+++ b/solution.py
@@ -362,7 +362,11 @@
             return tuple(new_tails)
 
         lax.fori_loop(
-            0, blocks, gather, tuple(jnp.zeros((8, LANES), jnp.float32) for _ in range(3))
+            0,
+            blocks,
+            gather,
+            tuple(jnp.zeros((8, LANES), jnp.float32) for _ in range(3)),
+            unroll=2,
         )
 
         def convolve(group, carry):
@@ -403,7 +407,7 @@
                 filtered[block, at, :] = total[block * fold : (block + 1) * fold]
             return carry
 
-        lax.fori_loop(0, per_chunk, convolve, 0)
+        lax.fori_loop(0, per_chunk, convolve, 0, unroll=2)
 
         def mix(block, carry):
             share, inner = block // slots, block % slots
@@ -417,7 +421,7 @@
                 back[chunk, a * shares + share, at, :] = returned[a * slot : (a + 1) * slot]
             return carry
 
-        lax.fori_loop(0, blocks, mix, 0)
+        lax.fori_loop(0, blocks, mix, 0, unroll=2)
 
     for chunk in range(chunks):
         others(lambda device: there(chunk, here, device).wait_recv())

time: 202 us -> 198 us (0.980); the launches traced: 200 us -> 198 us
  no operation moved by 1% of the time
where the time goes in v3:
time: 198 us
  Pallas kernels  192 us (97%)
  local copies, waits for them, and re-layouts  5.09 us (3%)
    pallas_call x1, Pallas kernels, channel_shards(): pl.pallas_call(functools.partial(channel_kernel, sizes), out_shape=jax.Sh...  192 us

profile of v3, /device:TPU:0, one launch (start us, length us, event | category | flops | bytes accessed | tf_op | source)
XLA Modules:
  0.0 198.0 jit_solution(15712085028174586847)
XLA Ops:
  0.0 0.8 fusion
  0.8 0.1 copy.28
  0.9 0.1 tile.9
  1.0 0.2 copy.24.coefficients
  1.2 0.2 copy.23.rates
  1.3 0.8 reshape.49
  2.2 0.1 reshape.50
  2.3 0.1 broadcast_subtract_fusion.order
  2.4 0.0 copy-start
  2.4 0.9 copy-done
  3.3 0.0 copy-start.1
  3.3 0.7 copy-done.1
  4.0 0.0 copy-start.2
  4.0 0.7 copy-done.2
  4.7 191.9 %shard_map.73 = bf16[128,8192]{1,0:T(8,128)(2,1)S(1)} custom-call(bf16[3,128,8192]{2,1,0:T(8,128)(2,1)} %projections.1, s32[16,1,256]{2,1,0:T(1,128)S(1)} %broadcast_subtract_fusion.order, s32[4]{0:T(128)S(1)} %copy-done.2, f32[3,3,4096]{2,1,0:T(4,128)S(1)} %copy-done, f32[1,4096]{1,0:T(1,128)S(1)} %bitcast.7, f32[16,16,1]{2,1,0:T(8,128)S(1)} %copy.23.rates, ...), custom_call_target="tpu_custom_call" | custom-call | tf_op jit(solution)/shard_map/pallas_call | solution.py:465
  196.7 1.3 copy.30
  (3 shorter events, 0.1 us)
Async XLA Ops:
  2.4 0.9 copy-start
  3.3 0.7 copy-start.1
  4.0 0.7 copy-start.2
